TPU v7x, 512 devices: a whole 4x4x16 slice. The times are simulated.
512 devices in a mesh: tm: 32 (over x_lo, z), gx: 16 (over x_hi, y, core).
Axes of the slice: x: 4 (x_hi: 2, x_lo: 2; x = x_hi * 2 + x_lo), y: 4, z: 16, core: 2. Of those that a mesh axis runs over, the one named last changes fastest.
Arguments:
- initial: float32 [32, 256, 256], P('gx'), may hold values from -1 to 1
- node_values: float32 [32, 3, 32, 256, 256], P('tm', None, 'gx'), may hold values from -1 to 1
Outputs:
- solution: float32 [32, 3, 32, 256, 256], P('tm', None, 'gx')
All inputs are finite; a program needn't handle non-finite values.
Results may differ from a plain program's by a relative error of at most 0.0002.
Values sent between devices are 32-bit elements; how exact they have to be, the bound alone decides.
A program may use at most 64 MiB of HBM per device.

v0:
```python
import math

import jax
import jax.numpy as jnp
from jax import lax
from jax.sharding import PartitionSpec as P

SWEEPS = 2


spacing = 2.0
step_size = 0.2
half_step = 0.1


def padded_2(cells, sides, width):
    for axis, dim in sides:
        count = lax.axis_size(axis)
        head = lax.slice_in_dim(cells, 0, width, axis=dim)
        tail = lax.slice_in_dim(cells, cells.shape[dim] - width, cells.shape[dim], axis=dim)
        cells = jnp.concatenate(
            [
                lax.ppermute(tail, axis, [(i, (i + 1) % count) for i in range(count)]),
                cells,
                lax.ppermute(head, axis, [((i + 1) % count, i) for i in range(count)]),
            ],
            axis=dim,
        )
    return cells


def passed_along(shard, axis, by):
    length = lax.axis_size(axis)
    pairs = [(i, i + by) for i in range(length) if 0 <= i + by < length]
    return lax.ppermute(shard, axis, pairs)


def second_derivative(count):
    positions = jnp.arange(count, dtype=jnp.int32)
    offset = positions[None, :] - positions[:, None]
    angle_step = 2.0 * math.pi / count
    parity = jnp.where(offset % 2 == 0, 1.0, -1.0).astype(jnp.float32)
    safe = jnp.where(offset == 0, 1, offset).astype(jnp.float32)
    sine_value = jnp.sin(safe * (angle_step / 2.0))
    off_value = -0.5 * parity / (sine_value * sine_value)
    diagonal_value = -math.pi**2 / (3.0 * angle_step * angle_step) - 1.0 / 6.0
    matrix = jnp.where(offset == 0, jnp.float32(diagonal_value), off_value)
    return matrix * (angle_step / spacing) ** 2


def evaluate(state_field, matrix_y, matrix_z):
    padded = padded_2(state_field, (("gx", 0),), 2)
    term_y = jnp.einsum("jk,xkz->xjz", matrix_y, state_field, precision=lax.Precision.HIGHEST)
    term_z = jnp.einsum("xyk,kz->xyz", state_field, matrix_z, precision=lax.Precision.HIGHEST)
    across = (
        -(padded[:-4] + padded[4:]) + 16.0 * (padded[1:-3] + padded[3:-1]) - 30.0 * state_field
    ) / 12.0
    return across + term_y + term_z + state_field - state_field * state_field * state_field


def local(initial, node_values):
    matrix_y = second_derivative(node_values.shape[3])
    matrix_z = second_derivative(node_values.shape[4])
    leading = lax.axis_index("tm") == 0
    values = [node_values[0, 0], node_values[0, 1], node_values[0, 2]]
    forces = [evaluate(item, matrix_y, matrix_z) for item in values]
    for sweep_index in range(SWEEPS):
        quadrature_one = step_size * (
            5.0 / 24.0 * forces[0] + 1.0 / 3.0 * forces[1] - 1.0 / 24.0 * forces[2]
        )
        quadrature_two = step_size * (
            -1.0 / 24.0 * forces[0] + 1.0 / 3.0 * forces[1] + 5.0 / 24.0 * forces[2]
        )
        arrived = passed_along(values[2], "tm", 1)
        first_node = jnp.where(leading, initial, arrived)
        first_force = evaluate(first_node, matrix_y, matrix_z)
        middle = first_node + half_step * (first_force - forces[0]) + quadrature_one
        middle_force = evaluate(middle, matrix_y, matrix_z)
        final_node = middle + half_step * (middle_force - forces[1]) + quadrature_two
        values = [first_node, middle, final_node]
        if sweep_index + 1 < SWEEPS:
            forces = [first_force, middle_force, evaluate(final_node, matrix_y, matrix_z)]
    return jnp.stack(values, axis=0)[None]


def solution(mesh):
    in_specs = (P("gx", None, None), P("tm", None, "gx", None, None))
    out_specs = P("tm", None, "gx", None, None)
    return jax.shard_map(local, mesh=mesh, in_specs=in_specs, out_specs=out_specs, check_vma=False)
```

profile of v0, /device:TPU:27, one launch (start us, length us, event | category | flops | bytes accessed | tf_op | source)
XLA Modules:
  0.0 152.3 jit_solution(16874535217749943801)
XLA Ops:
  2.5 4.0 %collective-permute-start.5 = (f32[2,256,256]{1,2,0:T(8,128)}, f32[2,256,256]{1,2,0:T(8,128)}, u32[]{:S(2)}, u32[]{:S(2)}) collective-permute-start(f32[2,256,256]{1,2,0:T(8,128)} %bitcast.132), channel_id=1, source_target_pairs={{0,1},{1,2},{2,3},{3,4},{4,5},{5,6},{6,7},{7,8},{8,9},{9,10},{10,1... | collective-permute-start | bytes 1572872 | tf_op jit(solution)/shard_map/ppermute | solution.py:23
  9.4 7.2 %collective-permute-start.3 = (f32[2,256,256]{1,2,0:T(8,128)}, f32[2,256,256]{1,2,0:T(8,128)}, u32[]{:S(2)}, u32[]{:S(2)}) collective-permute-start(f32[2,256,256]{1,2,0:T(8,128)} %bitcast.3), channel_id=1, source_target_pairs={{0,1},{1,2},{2,3},{3,4},{4,5},{5,6},{6,7},{7,8},{8,9},{9,10},{10,1... | collective-permute-start | bytes 1572872 | tf_op jit(solution)/shard_map/ppermute | solution.py:23
  18.8 3.5 %collective-permute-start = (f32[2,256,256]{1,2,0:T(8,128)S(1)}, f32[2,256,256]{1,2,0:T(8,128)}, u32[]{:S(2)}, u32[]{:S(2)}) collective-permute-start(f32[2,256,256]{1,2,0:T(8,128)S(1)} %bitcast.128), channel_id=1, source_target_pairs={{0,16},{16,32},{32,48},{48,64},{64,80},{80,96},{96,112},{112,128},... | collective-permute-start | bytes 1572872 | tf_op jit(solution)/shard_map/ppermute | solution.py:35
  22.3 2.7 %convolution_bitcast_fusion.7 = f32[2,256,256]{1,2,0:T(8,128)} fusion(f32[1,3,2,256,256]{4,3,2,1,0:T(8,128)S(1)} %copy-done), kind=kOutput, calls=%fused_computation.8 | convolution fusion | flops 404160512 | bytes 1048576 | tf_op jit(solution)/shard_map/jk,xkz->xjz/dot_general | solution.py:53
  25.0 2.7 %convolution_bitcast_fusion.9 = f32[2,256,256]{1,2,0:T(8,128)} fusion(f32[1,3,2,256,256]{4,3,2,1,0:T(8,128)S(1)} %copy-done), kind=kOutput, calls=%fused_computation.10 | convolution fusion | flops 404160512 | bytes 1048576 | tf_op jit(solution)/shard_map/jk,xkz->xjz/dot_general | solution.py:53
  29.8 9.2 %collective-permute-done = f32[2,256,256]{1,2,0:T(8,128)} collective-permute-done((f32[2,256,256]{1,2,0:T(8,128)S(1)}, f32[2,256,256]{1,2,0:T(8,128)}, u32[]{:S(2)}, u32[]{:S(2)}) %collective-permute-start) | collective-permute-done | bytes 524320 | tf_op jit(solution)/shard_map/ppermute | solution.py:35
  39.0 6.1 %collective-permute-start.7 = (f32[2,256,256]{1,2,0:T(8,128)S(1)}, f32[2,256,256]{1,2,0:T(8,128)S(1)}, u32[]{:S(2)}, u32[]{:S(2)}) collective-permute-start(f32[2,256,256]{1,2,0:T(8,128)S(1)} %bitcast.129), channel_id=1, source_target_pairs={{0,1},{1,2},{2,3},{3,4},{4,5},{5,6},{6,7},{7,8},{8,9},{9,10},{10,1... | collective-permute-start | bytes 1572872 | tf_op jit(solution)/shard_map/ppermute | solution.py:23
  46.3 2.1 %collective-permute-start.8 = (f32[2,256,256]{1,2,0:T(8,128)S(1)}, f32[2,256,256]{1,2,0:T(8,128)S(1)}, u32[]{:S(2)}, u32[]{:S(2)}) collective-permute-start(f32[2,256,256]{1,2,0:T(8,128)S(1)} %bitcast.130), channel_id=1, source_target_pairs={{1,0},{2,1},{3,2},{4,3},{5,4},{6,5},{7,6},{8,7},{9,8},{10,9},{11,1... | collective-permute-start | bytes 1572872 | tf_op jit(solution)/shard_map/ppermute | solution.py:25
  48.3 7.3 %collective-permute-start.1 = (f32[2,256,256]{1,2,0:T(8,128)S(1)}, f32[2,256,256]{1,2,0:T(8,128)S(1)}, u32[]{:S(2)}, u32[]{:S(2)}) collective-permute-start(f32[2,256,256]{1,2,0:T(8,128)S(1)} %broadcast_select_fusion.1), channel_id=1, source_target_pairs={{0,1},{1,2},{2,3},{3,4},{4,5},{5,6},{6,7},{7,8},{8,9},{9,10},{10,1... | collective-permute-start | bytes 1572872 | tf_op jit(solution)/shard_map/ppermute | solution.py:23
  55.6 3.5 %fusion.5 = f32[2,256,256]{1,2,0:T(8,128)S(1)} fusion(f32[2,256,256]{1,2,0:T(8,128)S(1)} %bitcast.134, f32[2,256,256]{1,2,0:T(8,128)S(1)} %copy-done.4, f32[2,256,256]{1,2,0:T(8,128)} %collective-permute-done.6, f32[2,256,256]{1,2,0:T(8,128)} %collective-permute-done.5, f32[1,3,2,256,256]{4,3,2,1,0:T(8,128)S(1)} %copy-done), kind=kOutput, calls=%fused_computation.17 | convolution fusion | flops 406257664 | bytes 3145728 | tf_op jit(solution)/shard_map/xyk,kz->xyz/dot_general | solution.py:54
  59.1 2.1 %collective-permute-start.2 = (f32[2,256,256]{1,2,0:T(8,128)S(1)}, f32[2,256,256]{1,2,0:T(8,128)S(1)}, u32[]{:S(2)}, u32[]{:S(2)}) collective-permute-start(f32[2,256,256]{1,2,0:T(8,128)S(1)} %broadcast_select_fusion.1), channel_id=1, source_target_pairs={{1,0},{2,1},{3,2},{4,3},{5,4},{6,5},{7,6},{8,7},{9,8},{10,9},{11,1... | collective-permute-start | bytes 1572872 | tf_op jit(solution)/shard_map/ppermute | solution.py:25
  61.3 3.9 %fusion.2 = f32[2,256,256]{1,2,0:T(8,128)S(1)} fusion(f32[2,256,256]{1,2,0:T(8,128)} %bitcast.3, f32[2,256,256]{1,2,0:T(8,128)S(1)} %copy-done.3, f32[2,256,256]{1,2,0:T(8,128)} %collective-permute-done.4, f32[2,256,256]{1,2,0:T(8,128)} %collective-permute-done.3, f32[1,3,2,256,256]{4,3,2,1,0:T(8,128)S(1)} %copy-done), kind=kOutput, calls=%fused_computation.14 | convolution fusion | flops 406257664 | bytes 3145728 | tf_op jit(solution)/shard_map/xyk,kz->xyz/dot_general | solution.py:54
  66.8 6.5 %collective-permute-done.2 = f32[2,256,256]{1,2,0:T(8,128)S(1)} collective-permute-done((f32[2,256,256]{1,2,0:T(8,128)S(1)}, f32[2,256,256]{1,2,0:T(8,128)S(1)}, u32[]{:S(2)}, u32[]{:S(2)}) %collective-permute-start.2) | collective-permute-done | bytes 524320 | tf_op jit(solution)/shard_map/ppermute | solution.py:25
  75.2 2.3 %multiply_add_fusion.1 = (f32[2,256,256]{1,2,0:T(8,128)S(1)}, f32[2,256,256]{1,2,0:T(8,128)S(1)}) fusion(f32[2,256,256]{1,2,0:T(8,128)S(1)} %fusion.2, f32[2,256,256]{1,2,0:T(8,128)S(1)} %broadcast_select_fusion.1, f32[2,256,256]{1,2,0:T(8,128)S(1)} %fusion.11, f32[2,256,256]{1,2,0:T(8,128)S(1)} %fusion.5, f32[2,256,256]{1,2,0:T(8,128)S(1)} %bitcast.131, ...), kind=kOutput, calls=%fused_computation.124 | convolution fusion | flops 407568384 | bytes 5767168 | tf_op jit(solution)/shard_map/xyk,kz->xyz/dot_general | solution.py:54
  79.5 7.5 %collective-permute-start.9 = (f32[2,256,256]{1,2,0:T(8,128)S(1)}, f32[2,256,256]{1,2,0:T(8,128)S(1)}, u32[]{:S(2)}, u32[]{:S(2)}) collective-permute-start(f32[2,256,256]{1,2,0:T(8,128)S(1)} %get-tuple-element.8), channel_id=1, source_target_pairs={{0,1},{1,2},{2,3},{3,4},{4,5},{5,6},{6,7},{7,8},{8,9},{9,10},{10,1... | collective-permute-start | bytes 1572872 | tf_op jit(solution)/shard_map/ppermute | solution.py:23
  88.6 3.1 %collective-permute-done.10 = f32[2,256,256]{1,2,0:T(8,128)S(1)} collective-permute-done((f32[2,256,256]{1,2,0:T(8,128)S(1)}, f32[2,256,256]{1,2,0:T(8,128)S(1)}, u32[]{:S(2)}, u32[]{:S(2)}) %collective-permute-start.10) | collective-permute-done | bytes 524320 | tf_op jit(solution)/shard_map/ppermute | solution.py:25
  92.8 2.1 %multiply_add_fusion = (f32[2,256,256]{1,2,0:T(8,128)S(1)}, f32[2,256,256]{1,2,0:T(8,128)S(1)}) fusion(f32[2,256,256]{1,2,0:T(8,128)S(1)} %get-tuple-element.9, f32[2,256,256]{1,2,0:T(8,128)S(1)} %fusion.2, f32[2,256,256]{1,2,0:T(8,128)S(1)} %get-tuple-element.8, f32[2,256,256]{1,2,0:T(8,128)S(1)} %fusion.5, ...), kind=kOutput, calls=%fused_computation.123 | convolution fusion | flops 407568384 | bytes 4718592 | tf_op jit(solution)/shard_map/xyk,kz->xyz/dot_general | solution.py:54
  96.8 8.0 %collective-permute-start.14 = (f32[2,256,256]{1,2,0:T(8,128)S(1)}, f32[2,256,256]{1,2,0:T(8,128)S(1)}, u32[]{:S(2)}, u32[]{:S(2)}) collective-permute-start(f32[2,256,256]{1,2,0:T(8,128)S(1)} %get-tuple-element.10), channel_id=1, source_target_pairs={{0,1},{1,2},{2,3},{3,4},{4,5},{5,6},{6,7},{7,8},{8,9},{9,10},{10,1... | collective-permute-start | bytes 1572872 | tf_op jit(solution)/shard_map/ppermute | solution.py:23
  108.5 7.8 %collective-permute-start.12 = (f32[2,256,256]{1,2,0:T(8,128)S(1)}, f32[2,256,256]{1,2,0:T(8,128)S(1)}, u32[]{:S(2)}, u32[]{:S(2)}) collective-permute-start(f32[2,256,256]{1,2,0:T(8,128)S(1)} %broadcast_select_fusion), channel_id=1, source_target_pairs={{0,1},{1,2},{2,3},{3,4},{4,5},{5,6},{6,7},{7,8},{8,9},{9,10},{10,1... | collective-permute-start | bytes 1572872 | tf_op jit(solution)/shard_map/ppermute | solution.py:23
  122.4 8.0 %collective-permute-done.13 = f32[2,256,256]{1,2,0:T(8,128)S(1)} collective-permute-done((f32[2,256,256]{1,2,0:T(8,128)S(1)}, f32[2,256,256]{1,2,0:T(8,128)S(1)}, u32[]{:S(2)}, u32[]{:S(2)}) %collective-permute-start.13) | collective-permute-done | bytes 524320 | tf_op jit(solution)/shard_map/ppermute | solution.py:25
  130.4 2.1 %fusion.17 = f32[2,256,256]{1,2,0:T(8,128)S(1)} fusion(f32[2,256,256]{1,2,0:T(8,128)S(1)} %broadcast_select_fusion, f32[2,256,256]{1,2,0:T(8,128)S(1)} %fusion.11, f32[2,256,256]{1,2,0:T(8,128)S(1)} %convolution_bitcast_fusion.2, f32[2,256,256]{1,2,0:T(8,128)S(1)} %collective-permute-done.13, f32[2,256,256]{1,2,0:T(8,128)S(1)} %collective-permute-done.12, ...), kind=kOutput, calls=%fused_computation.38 | convolution fusion | flops 407568384 | bytes 4194304 | tf_op jit(solution)/shard_map/xyk,kz->xyz/dot_general | solution.py:54
  134.4 2.7 %collective-permute-start.17 = (f32[2,256,256]{1,2,0:T(8,128)S(1)}, f32[2,256,256]{1,2,0:T(8,128)S(1)}, u32[]{:S(2)}, u32[]{:S(2)}) collective-permute-start(f32[2,256,256]{1,2,0:T(8,128)S(1)} %fusion.17), channel_id=1, source_target_pairs={{1,0},{2,1},{3,2},{4,3},{5,4},{6,5},{7,6},{8,7},{9,8},{10,9},{11,1... | collective-permute-start | bytes 1572872 | tf_op jit(solution)/shard_map/ppermute | solution.py:25
  140.5 8.0 %collective-permute-done.17 = f32[2,256,256]{1,2,0:T(8,128)S(1)} collective-permute-done((f32[2,256,256]{1,2,0:T(8,128)S(1)}, f32[2,256,256]{1,2,0:T(8,128)S(1)}, u32[]{:S(2)}, u32[]{:S(2)}) %collective-permute-start.17) | collective-permute-done | bytes 524320 | tf_op jit(solution)/shard_map/ppermute | solution.py:25
  148.5 2.1 %fusion.23 = f32[1,2,256,256]{2,3,1,0:T(8,128)S(1)} fusion(f32[2,256,256]{1,2,0:T(8,128)S(1)} %fusion.17, f32[2,256,256]{1,2,0:T(8,128)S(1)} %get-tuple-element.11, f32[2,256,256]{1,2,0:T(8,128)S(1)} %convolution_bitcast_fusion, f32[2,256,256]{1,2,0:T(8,128)S(1)} %collective-permute-done.17, f32[2,256,256]{1,2,0:T(8,128)S(1)} %collective-permute-done.16, ...), kind=kOutput, calls=%fused_computation.44 | convolution fusion | flops 407568384 | bytes 4194304 | tf_op jit(solution)/shard_map/xyk,kz->xyz/dot_general | solution.py:54
  (47 shorter events, 37.6 us)
Async XLA Ops:
  1.5 20.8 %copy-start = (f32[1,3,2,256,256]{4,3,2,1,0:T(8,128)S(1)}, f32[1,3,2,256,256]{4,3,2,1,0:T(8,128)}, u32[]{:S(2)}) copy-start(f32[1,3,2,256,256]{4,3,2,1,0:T(8,128)} %param.3) | copy-start | bytes 4718596
  2.5 43.8 %collective-permute-start.5 = (f32[2,256,256]{1,2,0:T(8,128)}, f32[2,256,256]{1,2,0:T(8,128)}, u32[]{:S(2)}, u32[]{:S(2)}) collective-permute-start(f32[2,256,256]{1,2,0:T(8,128)} %bitcast.132), channel_id=1, source_target_pairs={{0,1},{1,2},{2,3},{3,4},{4,5},{5,6},{6,7},{7,8},{8,9},{9,10},{10,1... | collective-permute-start | bytes 1572872 | tf_op jit(solution)/shard_map/ppermute | solution.py:23
  6.4 41.9 %collective-permute-start.6 = (f32[2,256,256]{1,2,0:T(8,128)}, f32[2,256,256]{1,2,0:T(8,128)}, u32[]{:S(2)}, u32[]{:S(2)}) collective-permute-start(f32[2,256,256]{1,2,0:T(8,128)} %bitcast.133), channel_id=1, source_target_pairs={{1,0},{2,1},{3,2},{4,3},{5,4},{6,5},{7,6},{8,7},{9,8},{10,9},{11,1... | collective-permute-start | bytes 1572872 | tf_op jit(solution)/shard_map/ppermute | solution.py:25
  9.4 49.8 %collective-permute-start.3 = (f32[2,256,256]{1,2,0:T(8,128)}, f32[2,256,256]{1,2,0:T(8,128)}, u32[]{:S(2)}, u32[]{:S(2)}) collective-permute-start(f32[2,256,256]{1,2,0:T(8,128)} %bitcast.3), channel_id=1, source_target_pairs={{0,1},{1,2},{2,3},{3,4},{4,5},{5,6},{6,7},{7,8},{8,9},{9,10},{10,1... | collective-permute-start | bytes 1572872 | tf_op jit(solution)/shard_map/ppermute | solution.py:23
  16.6 44.6 %collective-permute-start.4 = (f32[2,256,256]{1,2,0:T(8,128)}, f32[2,256,256]{1,2,0:T(8,128)}, u32[]{:S(2)}, u32[]{:S(2)}) collective-permute-start(f32[2,256,256]{1,2,0:T(8,128)} %bitcast.3), channel_id=1, source_target_pairs={{1,0},{2,1},{3,2},{4,3},{5,4},{6,5},{7,6},{8,7},{9,8},{10,9},{11,1... | collective-permute-start | bytes 1572872 | tf_op jit(solution)/shard_map/ppermute | solution.py:25
  18.8 20.3 %collective-permute-start = (f32[2,256,256]{1,2,0:T(8,128)S(1)}, f32[2,256,256]{1,2,0:T(8,128)}, u32[]{:S(2)}, u32[]{:S(2)}) collective-permute-start(f32[2,256,256]{1,2,0:T(8,128)S(1)} %bitcast.128), channel_id=1, source_target_pairs={{0,16},{16,32},{32,48},{48,64},{64,80},{80,96},{96,112},{112,128},... | collective-permute-start | bytes 1572872 | tf_op jit(solution)/shard_map/ppermute | solution.py:35
  25.0 2.7 %copy-start.1 = (f32[2,256,256]{2,1,0:T(8,128)S(1)}, f32[2,256,256]{2,1,0:T(8,128)}, u32[]{:S(2)}) copy-start(f32[2,256,256]{2,1,0:T(8,128)} %param.2) | copy-start | bytes 1572868
  27.9 27.7 %copy-start.2 = (f32[1,1,2,256,256]{3,4,2,1,0:T(8,128)S(1)}, f32[1,1,2,256,256]{3,4,2,1,0:T(8,128)}, u32[]{:S(2)}) copy-start(f32[1,1,2,256,256]{3,4,2,1,0:T(8,128)} %copy.58) | copy-start | bytes 1572868
  27.9 27.7 %copy-start.4 = (f32[2,256,256]{1,2,0:T(8,128)S(1)}, f32[2,256,256]{1,2,0:T(8,128)}, u32[]{:S(2)}) copy-start(f32[2,256,256]{1,2,0:T(8,128)} %convolution_bitcast_fusion.7) | copy-start | bytes 1572868
  39.0 36.1 %collective-permute-start.7 = (f32[2,256,256]{1,2,0:T(8,128)S(1)}, f32[2,256,256]{1,2,0:T(8,128)S(1)}, u32[]{:S(2)}, u32[]{:S(2)}) collective-permute-start(f32[2,256,256]{1,2,0:T(8,128)S(1)} %bitcast.129), channel_id=1, source_target_pairs={{0,1},{1,2},{2,3},{3,4},{4,5},{5,6},{6,7},{7,8},{8,9},{9,10},{10,1... | collective-permute-start | bytes 1572872 | tf_op jit(solution)/shard_map/ppermute | solution.py:23
  46.2 15.0 %copy-start.3 = (f32[2,256,256]{1,2,0:T(8,128)S(1)}, f32[2,256,256]{1,2,0:T(8,128)}, u32[]{:S(2)}) copy-start(f32[2,256,256]{1,2,0:T(8,128)} %convolution_bitcast_fusion.9) | copy-start | bytes 1572868
  46.3 28.9 %collective-permute-start.8 = (f32[2,256,256]{1,2,0:T(8,128)S(1)}, f32[2,256,256]{1,2,0:T(8,128)S(1)}, u32[]{:S(2)}, u32[]{:S(2)}) collective-permute-start(f32[2,256,256]{1,2,0:T(8,128)S(1)} %bitcast.130), channel_id=1, source_target_pairs={{1,0},{2,1},{3,2},{4,3},{5,4},{6,5},{7,6},{8,7},{9,8},{10,9},{11,1... | collective-permute-start | bytes 1572872 | tf_op jit(solution)/shard_map/ppermute | solution.py:25
  48.3 18.4 %collective-permute-start.1 = (f32[2,256,256]{1,2,0:T(8,128)S(1)}, f32[2,256,256]{1,2,0:T(8,128)S(1)}, u32[]{:S(2)}, u32[]{:S(2)}) collective-permute-start(f32[2,256,256]{1,2,0:T(8,128)S(1)} %broadcast_select_fusion.1), channel_id=1, source_target_pairs={{0,1},{1,2},{2,3},{3,4},{4,5},{5,6},{6,7},{7,8},{8,9},{9,10},{10,1... | collective-permute-start | bytes 1572872 | tf_op jit(solution)/shard_map/ppermute | solution.py:23
  59.1 14.1 %collective-permute-start.2 = (f32[2,256,256]{1,2,0:T(8,128)S(1)}, f32[2,256,256]{1,2,0:T(8,128)S(1)}, u32[]{:S(2)}, u32[]{:S(2)}) collective-permute-start(f32[2,256,256]{1,2,0:T(8,128)S(1)} %broadcast_select_fusion.1), channel_id=1, source_target_pairs={{1,0},{2,1},{3,2},{4,3},{5,4},{6,5},{7,6},{8,7},{9,8},{10,9},{11,1... | collective-permute-start | bytes 1572872 | tf_op jit(solution)/shard_map/ppermute | solution.py:25
  77.5 14.1 %collective-permute-start.10 = (f32[2,256,256]{1,2,0:T(8,128)S(1)}, f32[2,256,256]{1,2,0:T(8,128)S(1)}, u32[]{:S(2)}, u32[]{:S(2)}) collective-permute-start(f32[2,256,256]{1,2,0:T(8,128)S(1)} %get-tuple-element.8), channel_id=1, source_target_pairs={{1,0},{2,1},{3,2},{4,3},{5,4},{6,5},{7,6},{8,7},{9,8},{10,9},{11,1... | collective-permute-start | bytes 1572872 | tf_op jit(solution)/shard_map/ppermute | solution.py:25
  79.5 13.4 %collective-permute-start.9 = (f32[2,256,256]{1,2,0:T(8,128)S(1)}, f32[2,256,256]{1,2,0:T(8,128)S(1)}, u32[]{:S(2)}, u32[]{:S(2)}) collective-permute-start(f32[2,256,256]{1,2,0:T(8,128)S(1)} %get-tuple-element.8), channel_id=1, source_target_pairs={{0,1},{1,2},{2,3},{3,4},{4,5},{5,6},{6,7},{7,8},{8,9},{9,10},{10,1... | collective-permute-start | bytes 1572872 | tf_op jit(solution)/shard_map/ppermute | solution.py:23
  94.9 13.5 %collective-permute-start.11 = (f32[2,256,256]{1,2,0:T(8,128)S(1)}, f32[2,256,256]{1,2,0:T(8,128)S(1)}, u32[]{:S(2)}, u32[]{:S(2)}) collective-permute-start(f32[2,256,256]{1,2,0:T(8,128)S(1)} %get-tuple-element.10), channel_id=1, source_target_pairs={{0,16},{16,32},{32,48},{48,64},{64,80},{80,96},{96,112},{112,128},... | collective-permute-start | bytes 1572872 | tf_op jit(solution)/shard_map/ppermute | solution.py:35
  96.8 23.0 %collective-permute-start.14 = (f32[2,256,256]{1,2,0:T(8,128)S(1)}, f32[2,256,256]{1,2,0:T(8,128)S(1)}, u32[]{:S(2)}, u32[]{:S(2)}) collective-permute-start(f32[2,256,256]{1,2,0:T(8,128)S(1)} %get-tuple-element.10), channel_id=1, source_target_pairs={{0,1},{1,2},{2,3},{3,4},{4,5},{5,6},{6,7},{7,8},{8,9},{9,10},{10,1... | collective-permute-start | bytes 1572872 | tf_op jit(solution)/shard_map/ppermute | solution.py:23
  104.8 15.0 %collective-permute-start.15 = (f32[2,256,256]{1,2,0:T(8,128)S(1)}, f32[2,256,256]{1,2,0:T(8,128)S(1)}, u32[]{:S(2)}, u32[]{:S(2)}) collective-permute-start(f32[2,256,256]{1,2,0:T(8,128)S(1)} %get-tuple-element.10), channel_id=1, source_target_pairs={{1,0},{2,1},{3,2},{4,3},{5,4},{6,5},{7,6},{8,7},{9,8},{10,9},{11,1... | collective-permute-start | bytes 1572872 | tf_op jit(solution)/shard_map/ppermute | solution.py:25
  108.5 13.9 %collective-permute-start.12 = (f32[2,256,256]{1,2,0:T(8,128)S(1)}, f32[2,256,256]{1,2,0:T(8,128)S(1)}, u32[]{:S(2)}, u32[]{:S(2)}) collective-permute-start(f32[2,256,256]{1,2,0:T(8,128)S(1)} %broadcast_select_fusion), channel_id=1, source_target_pairs={{0,1},{1,2},{2,3},{3,4},{4,5},{5,6},{6,7},{7,8},{8,9},{9,10},{10,1... | collective-permute-start | bytes 1572872 | tf_op jit(solution)/shard_map/ppermute | solution.py:23
  116.3 14.1 %collective-permute-start.13 = (f32[2,256,256]{1,2,0:T(8,128)S(1)}, f32[2,256,256]{1,2,0:T(8,128)S(1)}, u32[]{:S(2)}, u32[]{:S(2)}) collective-permute-start(f32[2,256,256]{1,2,0:T(8,128)S(1)} %broadcast_select_fusion), channel_id=1, source_target_pairs={{1,0},{2,1},{3,2},{4,3},{5,4},{6,5},{7,6},{8,7},{9,8},{10,9},{11,1... | collective-permute-start | bytes 1572872 | tf_op jit(solution)/shard_map/ppermute | solution.py:25
  132.4 8.0 %collective-permute-start.16 = (f32[2,256,256]{1,2,0:T(8,128)S(1)}, f32[2,256,256]{1,2,0:T(8,128)S(1)}, u32[]{:S(2)}, u32[]{:S(2)}) collective-permute-start(f32[2,256,256]{1,2,0:T(8,128)S(1)} %fusion.17), channel_id=1, source_target_pairs={{0,1},{1,2},{2,3},{3,4},{4,5},{5,6},{6,7},{7,8},{8,9},{9,10},{10,1... | collective-permute-start | bytes 1572872 | tf_op jit(solution)/shard_map/ppermute | solution.py:23
  134.4 14.1 %collective-permute-start.17 = (f32[2,256,256]{1,2,0:T(8,128)S(1)}, f32[2,256,256]{1,2,0:T(8,128)S(1)}, u32[]{:S(2)}, u32[]{:S(2)}) collective-permute-start(f32[2,256,256]{1,2,0:T(8,128)S(1)} %fusion.17), channel_id=1, source_target_pairs={{1,0},{2,1},{3,2},{4,3},{5,4},{6,5},{7,6},{8,7},{9,8},{10,9},{11,1... | collective-permute-start | bytes 1572872 | tf_op jit(solution)/shard_map/ppermute | solution.py:25
where the time goes:
time: 153 us; the launch traced here: 152 us
  starting transfers between devices  71.6 us (47%)
  waiting for transfers between devices  38.5 us (25%)
  matrix products  35 us (23%)
  local copies, waits for them, and re-layouts  5.48 us (4%)
    ppermute x8, starting transfers between devices, padded_2(): lax.ppermute(tail, axis, [(i, (i + 1) % count) for i in range(count)])  49.7 us
    ppermute x8, waiting for transfers between devices, padded_2(): lax.ppermute(head, axis, [((i + 1) % count, i) for i in range(count)])  25.6 us
    dot_general x8, matrix products, evaluate(): jnp.einsum('xyk,kz->xyz', state_field, matrix_z, precision=lax.Precision....  19.7 us
    ppermute x8, starting transfers between devices, padded_2(): lax.ppermute(head, axis, [((i + 1) % count, i) for i in range(count)])  16.4 us
    dot_general x8, matrix products, evaluate(): jnp.einsum('jk,xkz->xjz', matrix_y, state_field, precision=lax.Precision....  15.3 us
    ppermute x2, waiting for transfers between devices, passed_along(): return lax.ppermute(shard, axis, pairs)  9.25 us
    ppermute x2, starting transfers between devices, passed_along(): return lax.ppermute(shard, axis, pairs)  5.47 us
    ppermute x8, waiting for transfers between devices, padded_2(): lax.ppermute(tail, axis, [(i, (i + 1) % count) for i in range(count)])  3.63 us
  transfers between devices with their start and end apart: 18, of which 8 were waited for; matrix products, arithmetic and copies ran while one was open for 19% of the time, Pallas kernels for 0%

commit v1 on v0

v1 whole, which is shorter than its diff:
```python
import math

import jax
import jax.numpy as jnp
import numpy as np
from jax import lax
from jax.experimental import pallas as pl
from jax.experimental.pallas import tpu as pltpu
from jax.sharding import PartitionSpec as P

MESH = pl.DeviceIdType.MESH

SPACING = 2.0
STEP = 0.2
HALF = 0.1
CHUNKS = 8

FIRST = (-HALF + STEP * 5.0 / 24.0, STEP / 3.0, -STEP / 24.0)
SECOND = (-STEP / 24.0, -HALF + STEP / 3.0, STEP * 5.0 / 24.0)


def second_derivative(count):
    positions = np.arange(count)
    offset = positions[None, :] - positions[:, None]
    angle_step = 2.0 * math.pi / count
    parity = np.where(offset % 2 == 0, 1.0, -1.0)
    safe = np.where(offset == 0, 1, offset)
    off_value = -0.5 * parity / np.sin(safe * (angle_step / 2.0)) ** 2
    diagonal = -(math.pi**2) / (3.0 * angle_step * angle_step) - 1.0 / 6.0
    return np.where(offset == 0, diagonal, off_value) * (angle_step / SPACING) ** 2


def split(x):
    high = x.astype(jnp.bfloat16)
    low = (x - high.astype(jnp.float32)).astype(jnp.bfloat16)
    return high, low


def dot(a, b):
    return jnp.dot(a, b, preferred_element_type=jnp.float32)


def reaction(v):
    return v - v * v * v


def kernel(
    nt,
    ng,
    initial,
    nodes,
    q_high,
    q_low,
    out,
    u0,
    u1,
    u2,
    a0,
    b0,
    w,
    halo,
    w_high,
    w_low,
    r1,
    m1,
    r2,
    m2,
    base,
    qterm,
    load_sem,
    start_sem,
    relay_send,
    relay_recv,
    halo_send,
    halo_recv,
    store_sem,
):
    t = lax.axis_index("tm")
    g = lax.axis_index("gx")
    right = lax.rem(g + 1, ng)
    left = lax.rem(g + ng - 1, ng)
    planes, ny, nz = u0.shape
    rows = ny // CHUNKS

    def part(c):
        return pl.ds(pl.multiple_of(c * rows, rows), rows)

    loads = [
        pltpu.make_async_copy(nodes.at[0, m], u, load_sem.at[m])
        for m, u in enumerate((u0, u1, u2))
    ]
    for load in loads:
        load.start()

    starts = [
        pltpu.make_async_copy(initial, a, start_sem.at[i])
        for i, a in enumerate((a0, b0))
    ]

    @pl.when(t == 0)
    def _():
        for start in starts:
            start.start()

    barrier = pltpu.get_barrier_semaphore()
    for side in (left, right):
        pl.semaphore_signal(barrier, inc=1, device_id=(t, side), device_id_type=MESH)

    @pl.when(t > 0)
    def _():
        pl.semaphore_signal(barrier, inc=1, device_id=(t - 1, g), device_id_type=MESH)

    pl.semaphore_wait(barrier, jnp.where(t < nt - 1, 3, 2))

    def relay(sweep, c):
        source = nodes.at[0, 2, :, part(c), :] if sweep == 0 else u2.at[:, part(c), :]
        target = (a0, b0)[sweep].at[:, part(c), :]
        return pltpu.make_async_remote_copy(
            source,
            target,
            relay_send.at[sweep, c],
            relay_recv.at[sweep, c],
            device_id=(t + 1, g),
            device_id_type=MESH,
        )

    def exchange(stage, side, c):
        return pltpu.make_async_remote_copy(
            w.at[stage, :, part(c), :],
            halo.at[stage, side, :, part(c), :],
            halo_send.at[stage, side, c],
            halo_recv.at[stage, side, c],
            device_id=(t, (right, left)[side]),
            device_id_type=MESH,
        )

    def loop(body):
        lax.fori_loop(0, CHUNKS, lambda c, _: (body(c), 0)[1], 0)

    @pl.when(t < nt - 1)
    def _():
        loop(lambda c: relay(0, c).start())

    for load in loads:
        load.wait()

    def prepare(c, first, middle, last):
        rhs = [reaction(first), reaction(middle), reaction(last)]
        old = (first, middle, last)
        at = (slice(None), part(c), slice(None))
        r1[at] = sum(k * v for k, v in zip(FIRST, old))
        m1[at] = sum(k * v for k, v in zip(FIRST, rhs))
        r2[at] = sum(k * v for k, v in zip(SECOND, old))
        m2[at] = sum(k * v for k, v in zip(SECOND, rhs))

    def across(stage, c):
        here = w[stage, :, part(c), :]
        before = halo[stage, 0, :, part(c), :]
        after = halo[stage, 1, :, part(c), :]
        one = 16.0 * (before[1] + here[1]) - 30.0 * here[0] - (before[0] + after[0])
        two = 16.0 * (here[0] + after[0]) - 30.0 * here[1] - (before[1] + after[1])
        return jnp.stack([one, two]) * (1.0 / 12.0)

    def offer(stage, c, value):
        w[stage, :, part(c), :] = value
        exchange(stage, 0, c).start()
        exchange(stage, 1, c).start()
        high, low = split(value)
        w_high[:, part(c), :] = high
        w_low[:, part(c), :] = low
        high = high.reshape(planes * rows, nz)
        low = low.reshape(planes * rows, nz)
        product = dot(high, q_high[...]) + dot(low, q_high[...]) + dot(high, q_low[...])
        qterm[:, part(c), :] = product.reshape(planes, rows, nz)

    def product_rows():
        for p in range(planes):
            qterm[p] += (
                dot(q_high[...], w_high[p])
                + dot(q_high[...], w_low[p])
                + dot(q_low[...], w_high[p])
            )

    def arrive(stage, c):
        exchange(stage, 0, c).wait_recv()
        exchange(stage, 1, c).wait_recv()

    loop(
        lambda c: prepare(
            c, u0[:, part(c), :], u1[:, part(c), :], u2[:, part(c), :]
        )
    )

    for sweep in range(2):
        begin = (a0, b0)[sweep]
        one, two = 2 * sweep, 2 * sweep + 1

        @pl.when(t == 0)
        def _():
            starts[sweep].wait()

        def take(c):
            @pl.when(t > 0)
            def _():
                relay(sweep, c).wait_recv()

            value = begin[:, part(c), :]
            base[:, part(c), :] = value + HALF * reaction(value) + m1[:, part(c), :]
            offer(one, c, HALF * value + r1[:, part(c), :])

        loop(take)
        if sweep == 1:
            pltpu.make_async_copy(b0, out.at[0, 0], store_sem.at[0]).start()
        product_rows()

        def middle(c):
            arrive(one, c)
            value = base[:, part(c), :] + qterm[:, part(c), :] + across(one, c)
            u1[:, part(c), :] = value
            base[:, part(c), :] = value + HALF * reaction(value) + m2[:, part(c), :]
            offer(two, c, HALF * value + r2[:, part(c), :])

        loop(middle)
        if sweep == 1:
            pltpu.make_async_copy(u1, out.at[0, 1], store_sem.at[1]).start()
        product_rows()

        def final(c):
            arrive(two, c)
            value = base[:, part(c), :] + qterm[:, part(c), :] + across(two, c)
            if sweep == 0:
                u2[:, part(c), :] = value

                @pl.when(t < nt - 1)
                def _():
                    relay(1, c).start()

                prepare(c, a0[:, part(c), :], u1[:, part(c), :], value)
            else:
                u0[:, part(c), :] = value

        if sweep == 0:

            @pl.when(t < nt - 1)
            def _():
                loop(lambda c: relay(0, c).wait_send())

        loop(final)

    last = pltpu.make_async_copy(u0, out.at[0, 2], store_sem.at[2])
    last.start()

    def drain(c):
        for stage in range(4):
            for side in range(2):
                exchange(stage, side, c).wait_send()

    loop(drain)

    @pl.when(t < nt - 1)
    def _():
        loop(lambda c: relay(1, c).wait_send())

    pltpu.make_async_copy(b0, out.at[0, 0], store_sem.at[0]).wait()
    pltpu.make_async_copy(u1, out.at[0, 1], store_sem.at[1]).wait()
    last.wait()


def solution(mesh):
    nt, ng = mesh.shape["tm"], mesh.shape["gx"]

    def local(initial, nodes):
        planes, ny, nz = initial.shape
        exact = second_derivative(ny).astype(np.float32)
        q_high = exact.astype(jnp.bfloat16)
        q_low = (exact - q_high.astype(np.float32)).astype(jnp.bfloat16)
        field = pltpu.VMEM((planes, ny, nz), jnp.float32)
        half_field = pltpu.VMEM((planes, ny, nz), jnp.bfloat16)
        dma = pltpu.SemaphoreType.DMA
        hbm = pl.BlockSpec(memory_space=pl.ANY)
        vmem = pl.BlockSpec(memory_space=pltpu.VMEM)

        def body(*refs):
            kernel(nt, ng, *refs)

        return pl.pallas_call(
            body,
            out_shape=jax.ShapeDtypeStruct(nodes.shape, nodes.dtype),
            in_specs=[hbm, hbm, vmem, vmem],
            out_specs=hbm,
            scratch_shapes=[
                field,
                field,
                field,
                field,
                field,
                pltpu.VMEM((4, planes, ny, nz), jnp.float32),
                pltpu.VMEM((4, 2, planes, ny, nz), jnp.float32),
                half_field,
                half_field,
                field,
                field,
                field,
                field,
                field,
                field,
                dma((3,)),
                dma((2,)),
                dma((2, CHUNKS)),
                dma((2, CHUNKS)),
                dma((4, 2, CHUNKS)),
                dma((4, 2, CHUNKS)),
                dma((3,)),
            ],
            compiler_params=pltpu.CompilerParams(
                collective_id=0,
                has_side_effects=True,
                vmem_limit_bytes=40 * 1024 * 1024,
            ),
            name="sweeps",
        )(initial, nodes, jnp.asarray(q_high), jnp.asarray(q_low))

    in_specs = (P("gx", None, None), P("tm", None, "gx", None, None))
    out_specs = P("tm", None, "gx", None, None)
    return jax.shard_map(
        local, mesh=mesh, in_specs=in_specs, out_specs=out_specs, check_vma=False
    )
```

time: 153 us -> 67.6 us (0.44)
  the two profiles are of different devices: /device:TPU:27 before, /device:TPU:29 now
where the time goes in v1:
time: 67.6 us; the launch traced here: 67.4 us
  Pallas kernels  62 us (92%)
  local copies, waits for them, and re-layouts  5.4 us (8%)
    pallas_call x1, Pallas kernels, local(): pl.pallas_call(body, out_shape=jax.ShapeDtypeStruct(nodes.shape, nodes.dt...  62 us
    unnamed x9, local copies, waits for them, and re-layouts  5.4 us

profile of v1, /device:TPU:29, one launch (start us, length us, event | category | flops | bytes accessed | tf_op | source)
XLA Modules:
  0.0 67.4 jit_solution(3880849991091289522)
XLA Ops:
  0.0 0.0 copy-start
  0.0 1.4 %copy-done = f32[1,3,2,256,256]{4,3,2,1,0:T(8,128)S(1)} copy-done((f32[1,3,2,256,256]{4,3,2,1,0:T(8,128)S(1)}, f32[1,3,2,256,256]{4,3,2,1,0:T(8,128)}, u32[]{:S(2)}) %copy-start) | copy-done | bytes 1572888
  1.4 0.0 copy-start.1
  1.4 1.0 %copy-done.1 = f32[2,256,256]{2,1,0:T(8,128)S(1)} copy-done((f32[2,256,256]{2,1,0:T(8,128)S(1)}, f32[2,256,256]{2,1,0:T(8,128)}, u32[]{:S(2)}) %copy-start.1) | copy-done | bytes 524312
  2.5 0.0 copy-start.2
  2.5 0.9 %copy-done.2 = bf16[256,256]{1,0:T(8,128)(2,1)S(1)} copy-done((bf16[256,256]{1,0:T(8,128)(2,1)S(1)}, bf16[256,256]{1,0:T(8,128)(2,1)}, u32[]{:S(2)}) %copy-start.2) | copy-done | bytes 131096
  3.4 0.0 copy-start.3
  3.4 0.9 %copy-done.3 = bf16[256,256]{1,0:T(8,128)(2,1)S(1)} copy-done((bf16[256,256]{1,0:T(8,128)(2,1)S(1)}, bf16[256,256]{1,0:T(8,128)(2,1)}, u32[]{:S(2)}) %copy-start.3) | copy-done | bytes 131096
  4.3 62.0 %sweeps.1 = f32[1,3,2,256,256]{4,3,2,1,0:T(8,128)S(1)} custom-call(f32[2,256,256]{2,1,0:T(8,128)S(1)} %copy-done.1, f32[1,3,2,256,256]{4,3,2,1,0:T(8,128)S(1)} %copy-done, bf16[256,256]{1,0:T(8,128)(2,1)S(1)} %copy-done.3, bf16[256,256]{1,0:T(8,128)(2,1)S(1)} %copy-done.2), custom_call_target="tpu_custom_call" | custom-call | tf_op jit(solution)/shard_map/sweeps/pallas_call | solution.py:286
  66.2 1.1 %copy.6 = f32[1,3,2,256,256]{4,3,2,1,0:T(8,128)} copy(f32[1,3,2,256,256]{4,3,2,1,0:T(8,128)S(1)} %sweeps.1) | data formatting | bytes 3145728
Async XLA Ops:
  0.0 1.4 %copy-start = (f32[1,3,2,256,256]{4,3,2,1,0:T(8,128)S(1)}, f32[1,3,2,256,256]{4,3,2,1,0:T(8,128)}, u32[]{:S(2)}) copy-start(f32[1,3,2,256,256]{4,3,2,1,0:T(8,128)} %refs_1_.1) | copy-start | bytes 4718596
  1.4 1.0 %copy-start.1 = (f32[2,256,256]{2,1,0:T(8,128)S(1)}, f32[2,256,256]{2,1,0:T(8,128)}, u32[]{:S(2)}) copy-start(f32[2,256,256]{2,1,0:T(8,128)} %refs_0_.1) | copy-start | bytes 1572868
  2.5 0.9 %copy-start.2 = (bf16[256,256]{1,0:T(8,128)(2,1)S(1)}, bf16[256,256]{1,0:T(8,128)(2,1)}, u32[]{:S(2)}) copy-start(bf16[256,256]{1,0:T(8,128)(2,1)} %constant.5.clone.refs_3_) | copy-start | bytes 393220
  3.4 0.9 %copy-start.3 = (bf16[256,256]{1,0:T(8,128)(2,1)S(1)}, bf16[256,256]{1,0:T(8,128)(2,1)}, u32[]{:S(2)}) copy-start(bf16[256,256]{1,0:T(8,128)(2,1)} %constant.4.clone.refs_2_) | copy-start | bytes 393220

commit v2 on v1

v2 whole, which is shorter than its diff:
```python
import math

import jax
import jax.numpy as jnp
import numpy as np
from jax import lax
from jax.experimental import pallas as pl
from jax.experimental.pallas import tpu as pltpu
from jax.sharding import PartitionSpec as P

MESH = pl.DeviceIdType.MESH

SPACING = 2.0
STEP = 0.2
HALF = 0.1
PARTS = 8
FINE = 8

FIRST = (-HALF + STEP * 5.0 / 24.0, STEP / 3.0, -STEP / 24.0)
SECOND = (-STEP / 24.0, -HALF + STEP / 3.0, STEP * 5.0 / 24.0)


def second_derivative(count):
    positions = np.arange(count)
    offset = positions[None, :] - positions[:, None]
    angle_step = 2.0 * math.pi / count
    parity = np.where(offset % 2 == 0, 1.0, -1.0)
    safe = np.where(offset == 0, 1, offset)
    off_value = -0.5 * parity / np.sin(safe * (angle_step / 2.0)) ** 2
    diagonal = -(math.pi**2) / (3.0 * angle_step * angle_step) - 1.0 / 6.0
    return np.where(offset == 0, diagonal, off_value) * (angle_step / SPACING) ** 2


def split(x):
    high = x.astype(jnp.bfloat16)
    low = (x - high.astype(jnp.float32)).astype(jnp.bfloat16)
    return high, low


def dot(a, b):
    return jnp.dot(a, b, preferred_element_type=jnp.float32)


def reaction(v):
    return v - v * v * v


def kernel(
    nt,
    ng,
    initial,
    nodes,
    q_high_in,
    q_low_in,
    out,
    u0,
    u1,
    u2,
    a0,
    b0,
    passing,
    w,
    halo,
    w_high,
    w_low,
    q_high,
    q_low,
    r1,
    m1,
    r2,
    m2,
    base,
    qterm,
    load_sem,
    start_sem,
    relay_send,
    relay_recv,
    pass_recv,
    halo_send,
    halo_recv,
):
    t = lax.axis_index("tm")
    g = lax.axis_index("gx")
    right = lax.rem(g + 1, ng)
    left = lax.rem(g + ng - 1, ng)
    planes, ny, nz = u0.shape
    rows, fine_rows = ny // PARTS, ny // FINE
    ratio = FINE // PARTS
    turn = nt // 2

    def part(c):
        return pl.ds(pl.multiple_of(c * rows, rows), rows)

    def fine(c):
        return pl.ds(pl.multiple_of(c * fine_rows, fine_rows), fine_rows)

    loads = [
        pltpu.make_async_copy(nodes.at[0, m], u, load_sem.at[m])
        for m, u in enumerate((u0, u1, u2))
    ]
    loads += [
        pltpu.make_async_copy(q_high_in, q_high, load_sem.at[3]),
        pltpu.make_async_copy(q_low_in, q_low, load_sem.at[4]),
    ]
    for load in loads:
        load.start()

    starts = [
        pltpu.make_async_copy(initial, a, start_sem.at[i])
        for i, a in enumerate((a0, b0))
    ]

    @pl.when(t == 0)
    def _():
        for start in starts:
            start.start()

    barrier = pltpu.get_barrier_semaphore()
    for side in (left, right):
        pl.semaphore_signal(barrier, inc=1, device_id=(t, side), device_id_type=MESH)

    @pl.when(t > 0)
    def _():
        pl.semaphore_signal(barrier, inc=1, device_id=(t - 1, g), device_id_type=MESH)

    @pl.when(t == turn)
    def _():
        pl.semaphore_signal(barrier, inc=1, device_id=(nt - 1, g), device_id_type=MESH)

    @pl.when(t == nt - 1)
    def _():
        pl.semaphore_signal(barrier, inc=1, device_id=(turn - 1, g), device_id_type=MESH)

    pl.semaphore_wait(barrier, jnp.where(t == turn - 1, 4, 3))

    def relay(sweep, c):
        source = nodes.at[0, 2, :, fine(c), :] if sweep == 0 else u2.at[:, fine(c), :]
        target = (a0, b0)[sweep].at[:, fine(c), :]
        return pltpu.make_async_remote_copy(
            source,
            target,
            relay_send.at[sweep, c],
            relay_recv.at[sweep, c],
            device_id=(t + 1, g),
            device_id_type=MESH,
        )

    def detour(sweep, c):
        source = nodes.at[0, 2, :, fine(c), :] if sweep == 0 else u2.at[:, fine(c), :]
        return pltpu.make_async_remote_copy(
            source,
            passing.at[sweep, :, fine(c), :],
            relay_send.at[sweep, c],
            pass_recv.at[sweep, c],
            device_id=(nt - 1, g),
            device_id_type=MESH,
        )

    def forward(sweep, c):
        return pltpu.make_async_remote_copy(
            passing.at[sweep, :, fine(c), :],
            (a0, b0)[sweep].at[:, fine(c), :],
            relay_send.at[sweep, c],
            relay_recv.at[sweep, c],
            device_id=(turn, g),
            device_id_type=MESH,
        )

    def aside(c):
        return (lax.rem(c, 2 * ratio) < ratio) & (c < 3 * FINE // 4)

    def give(sweep, c):
        around = (t == turn - 1) & aside(c)

        @pl.when(around)
        def _():
            detour(sweep, c).start()

        @pl.when((t < nt - 1) & ~around)
        def _():
            relay(sweep, c).start()

    def pass_on(sweep, k, due):
        @pl.when((t == nt - 1) & due)
        def _():
            for i in range(ratio):
                detour(sweep, k * ratio + i).wait_recv()
                forward(sweep, k * ratio + i).start()

    def given(sweep, c):
        @pl.when((t < nt - 1) | aside(c))
        def _():
            relay(sweep, c).wait_send()

    def exchange(stage, side, c):
        at = (part if stage % 2 else fine)(c)
        return pltpu.make_async_remote_copy(
            w.at[stage, :, at, :],
            halo.at[stage, side, :, at, :],
            halo_send.at[stage, side, c],
            halo_recv.at[stage, side, c],
            device_id=(t, (right, left)[side]),
            device_id_type=MESH,
        )

    def loop(body, count=PARTS):
        lax.fori_loop(0, count, lambda c, _: (body(c), 0)[1], 0)

    loop(lambda c: give(0, c), FINE)

    for load in loads:
        load.wait()

    def prepare(c, first, middle, last):
        rhs = [reaction(first), reaction(middle), reaction(last)]
        old = (first, middle, last)
        at = (slice(None), part(c), slice(None))
        r1[at] = sum(k * v for k, v in zip(FIRST, old))
        m1[at] = sum(k * v for k, v in zip(FIRST, rhs))
        r2[at] = sum(k * v for k, v in zip(SECOND, old))
        m2[at] = sum(k * v for k, v in zip(SECOND, rhs))

    def across(stage, c):
        here = w[stage, :, part(c), :]
        before = halo[stage, 0, :, part(c), :]
        after = halo[stage, 1, :, part(c), :]
        one = 16.0 * (before[1] + here[1]) - 30.0 * here[0] - (before[0] + after[0])
        two = 16.0 * (here[0] + after[0]) - 30.0 * here[1] - (before[1] + after[1])
        return jnp.stack([one, two]) * (1.0 / 12.0)

    def offer(stage, c, value):
        at = (part if stage % 2 else fine)(c)
        w[stage, :, at, :] = value
        exchange(stage, 0, c).start()
        exchange(stage, 1, c).start()
        high, low = split(value)
        w_high[:, at, :] = high
        w_low[:, at, :] = low

    def product_columns(c, count):
        at = pl.ds(pl.multiple_of(c * count, count), count)
        high = w_high[:, at, :].reshape(planes * count, nz)
        low = w_low[:, at, :].reshape(planes * count, nz)
        product = dot(high, q_high[...]) + dot(low, q_high[...]) + dot(high, q_low[...])
        qterm[:, at, :] = product.reshape(planes, count, nz)

    def product_rows():
        for p in range(planes):
            qterm[p] += (
                dot(q_high[...], w_high[p])
                + dot(q_high[...], w_low[p])
                + dot(q_low[...], w_high[p])
            )

    def arrive(stage, c):
        for i in [c] if stage % 2 else [ratio * c + i for i in range(ratio)]:
            exchange(stage, 0, i).wait_recv()
            exchange(stage, 1, i).wait_recv()

    loop(
        lambda c: prepare(
            c, u0[:, part(c), :], u1[:, part(c), :], u2[:, part(c), :]
        )
    )

    for sweep in range(2):
        begin = (a0, b0)[sweep]
        one, two = 2 * sweep, 2 * sweep + 1

        @pl.when(t == 0)
        def _():
            starts[sweep].wait()

        if sweep == 0:
            for k in range(0, 3 * PARTS // 4, 2):
                pass_on(0, k, True)

        def take(c):
            @pl.when(t > 0)
            def _():
                relay(sweep, c).wait_recv()

            value = begin[:, fine(c), :]
            if sweep == 1:
                out[0, 0, :, fine(c), :] = value
            base[:, fine(c), :] = value + HALF * reaction(value) + m1[:, fine(c), :]
            offer(one, c, HALF * value + r1[:, fine(c), :])
            product_columns(c, fine_rows)

        loop(take, FINE)
        product_rows()

        def middle(c):
            arrive(one, c)
            value = base[:, part(c), :] + qterm[:, part(c), :] + across(one, c)
            if sweep == 0:
                u1[:, part(c), :] = value
            else:
                out[0, 1, :, part(c), :] = value
            base[:, part(c), :] = value + HALF * reaction(value) + m2[:, part(c), :]
            offer(two, c, HALF * value + r2[:, part(c), :])

        loop(middle)
        product_columns(0, ny)
        product_rows()

        def final(c):
            if sweep == 0:
                pass_on(1, c - 4, (c >= 4) & (lax.rem(c, 2) == 0))
            arrive(two, c)
            value = base[:, part(c), :] + qterm[:, part(c), :] + across(two, c)
            if sweep == 0:
                u2[:, part(c), :] = value

                for i in range(ratio):
                    give(1, ratio * c + i)
                prepare(c, a0[:, part(c), :], u1[:, part(c), :], value)
            else:
                out[0, 2, :, part(c), :] = value

        if sweep == 0:
            loop(lambda c: given(0, c), FINE)

        loop(final)
        if sweep == 0:
            pass_on(1, PARTS - 4, True)

    for stage in range(4):

        def drain(c):
            exchange(stage, 0, c).wait_send()
            exchange(stage, 1, c).wait_send()

        loop(drain, PARTS if stage % 2 else FINE)

    loop(lambda c: given(1, c), FINE)


def solution(mesh):
    nt, ng = mesh.shape["tm"], mesh.shape["gx"]

    def local(initial, nodes):
        planes, ny, nz = initial.shape
        exact = second_derivative(ny).astype(np.float32)
        q_high = exact.astype(jnp.bfloat16)
        q_low = (exact - q_high.astype(np.float32)).astype(jnp.bfloat16)
        field = pltpu.VMEM((planes, ny, nz), jnp.float32)
        half_field = pltpu.VMEM((planes, ny, nz), jnp.bfloat16)
        dma = pltpu.SemaphoreType.DMA
        hbm = pl.BlockSpec(memory_space=pl.ANY)

        def body(*refs):
            kernel(nt, ng, *refs)

        return pl.pallas_call(
            body,
            out_shape=jax.ShapeDtypeStruct(nodes.shape, nodes.dtype),
            in_specs=[hbm, hbm, hbm, hbm],
            out_specs=pl.BlockSpec(memory_space=pltpu.VMEM),
            scratch_shapes=[
                field,
                field,
                field,
                field,
                field,
                pltpu.VMEM((2, planes, ny, nz), jnp.float32),
                pltpu.VMEM((4, planes, ny, nz), jnp.float32),
                pltpu.VMEM((4, 2, planes, ny, nz), jnp.float32),
                half_field,
                half_field,
                pltpu.VMEM((ny, ny), jnp.bfloat16),
                pltpu.VMEM((ny, ny), jnp.bfloat16),
                field,
                field,
                field,
                field,
                field,
                field,
                dma((5,)),
                dma((2,)),
                dma((2, FINE)),
                dma((2, FINE)),
                dma((2, FINE)),
                dma((4, 2, FINE)),
                dma((4, 2, FINE)),
            ],
            compiler_params=pltpu.CompilerParams(
                collective_id=0,
                has_side_effects=True,
                vmem_limit_bytes=24 * 1024 * 1024,
            ),
            name="sweeps",
        )(*(pltpu.with_memory_space_constraint(x, pltpu.HBM) for x in (initial, nodes, jnp.asarray(q_high), jnp.asarray(q_low))))

    in_specs = (P("gx", None, None), P("tm", None, "gx", None, None))
    out_specs = P("tm", None, "gx", None, None)
    return jax.shard_map(
        local, mesh=mesh, in_specs=in_specs, out_specs=out_specs, check_vma=False
    )
```

time: 67.6 us -> 56.8 us (0.84)
  the two profiles are of different devices: /device:TPU:29 before, /device:TPU:27 now
where the time goes in v2:
time: 56.8 us; the launch traced here: 56.7 us
  Pallas kernels  55.5 us (98%)
  local copies, waits for them, and re-layouts  1.15 us (2%)
    pallas_call x1, Pallas kernels, local(): pl.pallas_call(body, out_shape=jax.ShapeDtypeStruct(nodes.shape, nodes.dt...  55.5 us
    unnamed x1, local copies, waits for them, and re-layouts  1.15 us

profile of v2, /device:TPU:27, one launch (start us, length us, event | category | flops | bytes accessed | tf_op | source)
XLA Modules:
  0.0 56.7 jit_solution(17497198675170613906)
XLA Ops:
  0.0 55.5 %sweeps.1 = f32[1,3,2,256,256]{4,3,2,1,0:T(8,128)S(1)} custom-call(f32[2,256,256]{2,1,0:T(8,128)} %refs_0_.1, f32[1,3,2,256,256]{4,3,2,1,0:T(8,128)} %refs_1_.1, bf16[256,256]{1,0:T(8,128)(2,1)} %constant.4.clone.refs_2_, bf16[256,256]{1,0:T(8,128)(2,1)} %constant.5.clone.refs_3_), custom_call_target="tpu_custom_call" | custom-call | tf_op jit(solution)/shard_map/sweeps/pallas_call | solution.py:355
  55.5 1.1 %copy.6 = f32[1,3,2,256,256]{4,3,2,1,0:T(8,128)} copy(f32[1,3,2,256,256]{4,3,2,1,0:T(8,128)S(1)} %sweeps.1) | data formatting | bytes 3145728

commit v3 on v2

--- a/solution.py
+++ b/solution.py
@@ -14,6 +14,7 @@
 STEP = 0.2
 HALF = 0.1
 PARTS = 8
+AROUND = ((0, 1, 3), (1,))
 FINE = 8
 
 FIRST = (-HALF + STEP * 5.0 / 24.0, STEP / 3.0, -STEP / 24.0)
@@ -166,11 +167,14 @@
             device_id_type=MESH,
         )
 
-    def aside(c):
-        return (lax.rem(c, 2 * ratio) < ratio) & (c < 3 * FINE // 4)
+    def aside(sweep, c):
+        found = c == -99
+        for k in AROUND[sweep]:
+            found = found | (c == k)
+        return found
 
     def give(sweep, c):
-        around = (t == turn - 1) & aside(c)
+        around = (t == turn - 1) & aside(sweep, c)
 
         @pl.when(around)
         def _():
@@ -188,7 +192,7 @@
                 forward(sweep, k * ratio + i).start()
 
     def given(sweep, c):
-        @pl.when((t < nt - 1) | aside(c))
+        @pl.when((t < nt - 1) | aside(sweep, c))
         def _():
             relay(sweep, c).wait_send()
 
@@ -272,7 +276,7 @@
             starts[sweep].wait()
 
         if sweep == 0:
-            for k in range(0, 3 * PARTS // 4, 2):
+            for k in AROUND[0]:
                 pass_on(0, k, True)
 
         def take(c):
@@ -306,7 +310,7 @@
 
         def final(c):
             if sweep == 0:
-                pass_on(1, c - 4, (c >= 4) & (lax.rem(c, 2) == 0))
+                pass_on(1, c - 4, aside(1, c - 4))
             arrive(two, c)
             value = base[:, part(c), :] + qterm[:, part(c), :] + across(two, c)
             if sweep == 0:
@@ -323,7 +327,9 @@
 
         loop(final)
         if sweep == 0:
-            pass_on(1, PARTS - 4, True)
+            for k in AROUND[1]:
+                if k >= PARTS - 4:
+                    pass_on(1, k, True)
 
     for stage in range(4):
 

time: 56.8 us -> 55.4 us (0.975)
  the two profiles are of different devices: /device:TPU:27 before, /device:TPU:29 now
where the time goes in v3:
time: 55.4 us; the launch traced here: 55.2 us
  Pallas kernels  54.1 us (98%)
  local copies, waits for them, and re-layouts  1.15 us (2%)
    pallas_call x1, Pallas kernels, local(): pl.pallas_call(body, out_shape=jax.ShapeDtypeStruct(nodes.shape, nodes.dt...  54.1 us
    unnamed x1, local copies, waits for them, and re-layouts  1.15 us

profile of v3, /device:TPU:29, one launch (start us, length us, event | category | flops | bytes accessed | tf_op | source)
XLA Modules:
  0.0 55.2 jit_solution(3371463150491312905)
XLA Ops:
  0.0 54.1 %sweeps.1 = f32[1,3,2,256,256]{4,3,2,1,0:T(8,128)S(1)} custom-call(f32[2,256,256]{2,1,0:T(8,128)} %refs_0_.1, f32[1,3,2,256,256]{4,3,2,1,0:T(8,128)} %refs_1_.1, bf16[256,256]{1,0:T(8,128)(2,1)} %constant.4.clone.refs_2_, bf16[256,256]{1,0:T(8,128)(2,1)} %constant.5.clone.refs_3_), custom_call_target="tpu_custom_call" | custom-call | tf_op jit(solution)/shard_map/sweeps/pallas_call | solution.py:361
  54.1 1.1 %copy.6 = f32[1,3,2,256,256]{4,3,2,1,0:T(8,128)} copy(f32[1,3,2,256,256]{4,3,2,1,0:T(8,128)S(1)} %sweeps.1) | data formatting | bytes 3145728

commit v4 on v3

--- a/solution.py
+++ b/solution.py
@@ -14,7 +14,7 @@
 STEP = 0.2
 HALF = 0.1
 PARTS = 8
-AROUND = ((0, 1, 3), (1,))
+AROUND = ((0, 1, 2, 3), (1,))
 FINE = 8
 
 FIRST = (-HALF + STEP * 5.0 / 24.0, STEP / 3.0, -STEP / 24.0)

time: 55.4 us -> 55.4 us (level)
  no operation moved by 1% of the time
where the time goes in v4:
time: 55.4 us; the launch traced here: 55.2 us
  Pallas kernels  54.1 us (98%)
  local copies, waits for them, and re-layouts  1.15 us (2%)
    pallas_call x1, Pallas kernels, local(): pl.pallas_call(body, out_shape=jax.ShapeDtypeStruct(nodes.shape, nodes.dt...  54.1 us
    unnamed x1, local copies, waits for them, and re-layouts  1.15 us

profile of v4, /device:TPU:29, one launch (start us, length us, event | category | flops | bytes accessed | tf_op | source)
XLA Modules:
  0.0 55.2 jit_solution(5635444220140331700)
XLA Ops:
  0.0 54.1 %sweeps.1 = f32[1,3,2,256,256]{4,3,2,1,0:T(8,128)S(1)} custom-call(f32[2,256,256]{2,1,0:T(8,128)} %refs_0_.1, f32[1,3,2,256,256]{4,3,2,1,0:T(8,128)} %refs_1_.1, bf16[256,256]{1,0:T(8,128)(2,1)} %constant.4.clone.refs_2_, bf16[256,256]{1,0:T(8,128)(2,1)} %constant.5.clone.refs_3_), custom_call_target="tpu_custom_call" | custom-call | tf_op jit(solution)/shard_map/sweeps/pallas_call | solution.py:361
  54.1 1.1 %copy.6 = f32[1,3,2,256,256]{4,3,2,1,0:T(8,128)} copy(f32[1,3,2,256,256]{4,3,2,1,0:T(8,128)S(1)} %sweeps.1) | data formatting | bytes 3145728
